TPU v7x, 32 devices: a whole 2x2x4 slice. The times are simulated.
32 devices in a mesh: parts: 2 (over y), node: 4 (over z), chan: 2 (over x), rep: 2 (over core).
Axes of the slice: x: 2, y: 2, z: 4, core: 2. Of those that a mesh axis runs over, the one named last changes fastest.
Arguments:
- features: float32 [128, 32768], P('chan', ('parts', 'node')), parts along dimension 1, may hold values from -6 to 6
- tile_rows: int32 [2048], P(('parts', 'node', 'rep')), parts along dimension 0, may hold values from 0 to 31
- tile_slot: int32 [2048], P(('parts', 'node', 'rep')), parts along dimension 0, may hold values from 0 to 23, as said below
- slot_block: int32 [16, 24], P(('parts', 'node', 'rep')), parts along dimension 0, may hold values from -1 to 11, as said below
- tiles: int32 [2048, 8, 128], P(('parts', 'node', 'rep')), parts along dimension 0, may hold values from 0 to 65535, as said below
Outputs:
- propagated: float32 [128, 32768], P('chan', ('parts', 'node')), parts along dimension 1
There are 2 independent parts, one for each index of `parts`. A program takes and returns all parts, laid end to end along the dimension named above; each array names one. Nothing has to cross between parts.
Inputs may be any that keep to these rules, and one draw needn't show every extreme that they name: tile_slot // 6 is the owning node index of the tile's hyperedge block; slot_block of the tile's device at that slot is never -1. `slot_block`: for each device and owner, the live slots come first and name different blocks; -1 marks an unused slot; every device's slots for its own node index are all live. `tiles`: word w of column j holds node 16 * w + k in bit k.
All inputs are finite; a program needn't handle non-finite values.
Results may differ from a plain program's by a relative error of at most 0.0001.
Values sent between devices are 32-bit elements; how exact they have to be, the bound alone decides.
A program may use at most 64 MiB of HBM per device.

v0:
```python
import functools

import jax
import jax.numpy as jnp
from jax import lax
from jax.experimental import pallas as pl
from jax.experimental.pallas import tpu as pltpu
from jax.sharding import PartitionSpec as P

EB_DEV = 12
CAP = 6
ROUNDS = 2
CHUNKS = 8
OUT_CHUNKS = 4
UNROLL = 8
MESH = pl.DeviceIdType.MESH
teleport = 0.1


def split_rows(value, ones):
    high = value.astype(jnp.bfloat16).astype(jnp.float32)
    parts = [high, value - high]
    if ones:
        parts.append(jnp.ones((16, 128), jnp.float32))
    return jnp.concatenate(parts, axis=0).astype(jnp.bfloat16)


def kernel(
    n_node,
    order_e, row_e, keep_e, last_e, order_r, edge_r, keep_r, last_r,
    feat_ref, tiles_ref,
    out_ref,
    tiles_in, unp, xs, ms, run_sums, own, in_left, in_right, to_left, to_right,
    own_deg, deg_left, deg_right, deg_to_left, deg_to_right, node_floor, edge_inv,
    tile_sem, out_send, out_recv, send_l, send_r, recv_l, recv_r, deg_sem,
):
    ch = feat_ref.shape[1]
    tile_count = tiles_ref.shape[0]
    total_tiles = 2 * tile_count
    nblocks = feat_ref.shape[2] // 128
    edge_blocks = own.shape[0]
    per = edge_blocks // CHUNKS
    pos = lax.axis_index("node")
    rep = lax.axis_index("rep")
    left, right = pos - 1, pos + 1
    has_left = pos > 0
    has_right = pos < n_node - 1

    barrier = pltpu.get_barrier_semaphore()
    pl.semaphore_signal(barrier, inc=1, device_id={"rep": 1 - rep}, device_id_type=MESH)

    @pl.when(has_left)
    def _():
        pl.semaphore_signal(barrier, inc=1, device_id={"node": left}, device_id_type=MESH)

    @pl.when(has_right)
    def _():
        pl.semaphore_signal(barrier, inc=1, device_id={"node": right}, device_id_type=MESH)

    pl.semaphore_wait(barrier, 1 + jnp.where(has_left, 1, 0) + jnp.where(has_right, 1, 0))

    tile_copy = pltpu.make_async_remote_copy(
        src_ref=tiles_ref, dst_ref=tiles_in, send_sem=tile_sem.at[0], recv_sem=tile_sem.at[1],
        device_id={"rep": 1 - rep}, device_id_type=MESH,
    )
    tile_copy.start()

    zero_rows = jnp.zeros(run_sums.shape[1:], jnp.float32)
    run_sums[total_tiles] = zero_rows
    bit = jnp.left_shift(1, lax.broadcasted_iota(jnp.int32, (128, 128), 0) & 15)

    def unpack_from(source, base):
        def body(t, _):
            packed = source[t]
            words = jnp.broadcast_to(packed[:, None, :], (8, 16, 128)).reshape(128, 128)
            ones = jnp.where((words & bit) != 0, 1.0, 0.0)
            unp[base + t] = ones.astype(jnp.bfloat16)
            return 0

        lax.fori_loop(0, tile_count, body, 0, unroll=4)

    def load_features(r, _):
        block = feat_ref[rep, :, pl.ds(pl.multiple_of(r * 128, 128), 128)]
        xs[r] = split_rows(block, True)
        return 0

    lax.fori_loop(0, nblocks, load_features, 0, unroll=2)
    unpack_from(tiles_ref, 0)
    tile_copy.wait()
    unpack_from(tiles_in, tile_count)

    def sweep(order, source_of, keep, source, transposed, first):
        rows = 2 * ch + (16 if first else 0)
        dims = (((1,), (1 if transposed else 0,)), ((), ()))

        def step(t, running):
            product = lax.dot_general(
                source[source_of[t]][:rows], unp[order[t]], dims,
                preferred_element_type=jnp.float32,
            )
            fresh = product[:ch] + product[ch:2 * ch]
            if first:
                fresh = jnp.concatenate([fresh, product[2 * ch:2 * ch + 8]], axis=0)
            running = running * keep[t] + fresh
            run_sums[t, :ch + (8 if first else 0)] = running
            return running

        start = jnp.zeros((ch + (8 if first else 0), 128), jnp.float32)
        lax.fori_loop(0, total_tiles, step, start, unroll=UNROLL)

    def remote(source, target, send, recv, where):
        return pltpu.make_async_remote_copy(
            src_ref=source, dst_ref=target, send_sem=send, recv_sem=recv,
            device_id={"node": where}, device_id_type=MESH,
        )

    def chunk_copies(turn, k):
        part = pl.ds(k * per, per)
        go_right = remote(to_right.at[turn, part], in_left.at[turn, part],
                          send_r.at[turn, k], recv_l.at[turn, k], right)
        go_left = remote(to_left.at[turn, part], in_right.at[turn, part],
                         send_l.at[turn, k], recv_r.at[turn, k], left)
        return part, go_right, go_left

    def zero_ends(turn):
        @pl.when(jnp.logical_not(has_left))
        def _():
            in_left[turn] = jnp.zeros(in_left.shape[1:], jnp.float32)
            deg_left[...] = jnp.zeros_like(deg_left)

        @pl.when(jnp.logical_not(has_right))
        def _():
            in_right[turn] = jnp.zeros(in_right.shape[1:], jnp.float32)
            deg_right[...] = jnp.zeros_like(deg_right)

    def forward(turn, k):
        part, go_right, go_left = chunk_copies(turn, k)

        @pl.when(has_left)
        def _():
            go_right.wait_recv()

        @pl.when(has_right)
        def _():
            to_right[turn, part] = own[part] + in_left[turn, part]
            go_right.start()
            go_left.wait_recv()

        @pl.when(has_left)
        def _():
            to_left[turn, part] = own[part] + in_right[turn, part]
            go_left.start()

    def forward_degrees():
        go_right = remote(deg_to_right, deg_left, deg_sem.at[0], deg_sem.at[1], right)
        go_left = remote(deg_to_left, deg_right, deg_sem.at[2], deg_sem.at[3], left)

        @pl.when(has_left)
        def _():
            go_right.wait_recv()

        @pl.when(has_right)
        def _():
            deg_to_right[...] = own_deg[...] + deg_left[...]
            go_right.start()
            go_left.wait_recv()

        @pl.when(has_left)
        def _():
            deg_to_left[...] = own_deg[...] + deg_right[...]
            go_left.start()

        degree = own_deg[...] + deg_left[...] + deg_right[...]
        edge_inv[...] = 1.0 / jnp.maximum(degree, 1.0)

        @pl.when(has_right)
        def _():
            go_right.wait_send()

        @pl.when(has_left)
        def _():
            go_left.wait_send()

    for turn in range(ROUNDS):
        first = turn == 0
        zero_ends(turn)
        sweep(order_e, row_e, keep_e, xs, False, first)

        def take_edges(b, _, first=first):
            found = run_sums[last_e[b]]
            own[b] = found[:ch]
            if first:
                own_deg[b] = found[ch:ch + 8]
            return 0

        lax.fori_loop(0, edge_blocks, take_edges, 0, unroll=4)
        if first:
            forward_degrees()
        for k in range(CHUNKS):
            forward(turn, k)

        def means(b, _, turn=turn, first=first):
            edge_sum = own[b] + in_left[turn, b] + in_right[turn, b]
            ms[b] = split_rows(edge_sum * edge_inv[b, :1], True)
            return 0

        lax.fori_loop(0, edge_blocks, means, 0, unroll=2)
        ms[edge_blocks] = jnp.concatenate(
            [jnp.zeros((2 * ch, 128), jnp.float32), jnp.ones((16, 128), jnp.float32)], axis=0
        ).astype(jnp.bfloat16)

        for k in range(CHUNKS):
            part, go_right, go_left = chunk_copies(turn, k)

            @pl.when(has_right)
            def _():
                go_right.wait_send()

            @pl.when(has_left)
            def _():
                go_left.wait_send()

        sweep(order_r, edge_r, keep_r, ms, True, first)

        def new_block(r, first=first):
            found = run_sums[last_r[r]]
            if first:
                node_floor[r] = jnp.maximum(found[ch:ch + 8], 1.0)
            lanes = pl.ds(pl.multiple_of(r * 128, 128), 128)
            block = feat_ref[rep, :, lanes]
            return lanes, (1.0 - teleport) * (found[:ch] / node_floor[r][:1]) + teleport * block

        if turn < ROUNDS - 1:
            def next_x(r, _):
                xs[r] = split_rows(new_block(r)[1], True)
                return 0

            lax.fori_loop(0, nblocks, next_x, 0, unroll=2)
        else:
            group = nblocks // OUT_CHUNKS
            copies = []
            for k in range(OUT_CHUNKS):
                def last_x(r, _):
                    lanes, value = new_block(r)
                    out_ref[rep, :, lanes] = value
                    return 0

                lax.fori_loop(k * group, (k + 1) * group, last_x, 0, unroll=2)
                span = pl.ds(k * group * 128, group * 128)
                copy = pltpu.make_async_remote_copy(
                    src_ref=out_ref.at[rep, :, span], dst_ref=out_ref.at[rep, :, span],
                    send_sem=out_send.at[k], recv_sem=out_recv.at[k],
                    device_id={"rep": 1 - rep}, device_id_type=MESH,
                )
                copy.start()
                copies.append(copy)
            for copy in copies:
                copy.wait()


def shards(features, tile_rows, tile_slot, slot_block, tiles):
    n_node = lax.axis_size("node")
    channels, row_count = features.shape
    nblocks = row_count // 128
    tile_count = tile_rows.shape[0]
    total = 2 * tile_count
    ch = channels // 2
    edge_blocks = n_node * EB_DEV

    slots = slot_block.reshape(-1)
    slot_of = jnp.arange(slots.shape[0], dtype=jnp.int32)
    slot_edge = jnp.where(slots >= 0, slot_of // CAP * EB_DEV + slots, edge_blocks)
    edges = jnp.sum(jnp.where(tile_slot[:, None] == slot_of[None, :], slot_edge[None, :], 0), axis=1)
    mine = jnp.concatenate([tile_rows, edges.astype(jnp.int32)])
    theirs = lax.ppermute(mine, "rep", [(0, 1), (1, 0)])
    rows = jnp.concatenate([mine[:tile_count], theirs[:tile_count]])
    edges = jnp.concatenate([mine[tile_count:], theirs[tile_count:]])
    ids = jnp.arange(total, dtype=jnp.int32)

    def arrange(key, other, groups):
        full = key * total + ids
        rank = jnp.sum((full[None, :] < full[:, None]).astype(jnp.int32), axis=1)
        hot = rank[None, :] == ids[:, None]
        order = jnp.sum(jnp.where(hot, ids[None, :], 0), axis=1)
        source = jnp.sum(jnp.where(hot, other[None, :], 0), axis=1)
        first = jnp.sum((key[None, :] == key[:, None]) & (full[None, :] < full[:, None]), axis=1) == 0
        keep = jnp.sum(jnp.where(hot & ~first[None, :], 1.0, 0.0), axis=1)
        group = jnp.arange(groups, dtype=jnp.int32)
        upto = jnp.sum((key[None, :] <= group[:, None]).astype(jnp.int32), axis=1)
        some = jnp.any(key[None, :] == group[:, None], axis=1)
        return order, source, keep, jnp.where(some, upto - 1, total)

    order_e, row_e, keep_e, last_e = arrange(edges, rows, edge_blocks)
    order_r, edge_r, keep_r, last_r = arrange(rows, edges, nblocks)

    smem = pl.BlockSpec(memory_space=pltpu.SMEM)
    vmem = pl.BlockSpec(memory_space=pltpu.VMEM)
    f32, bf16 = jnp.float32, jnp.bfloat16
    wide = (edge_blocks, ch, 128)
    deg = (edge_blocks, 8, 128)
    dma = pltpu.SemaphoreType.DMA
    out = pl.pallas_call(
        functools.partial(kernel, n_node),
        out_shape=jax.ShapeDtypeStruct((2, ch, row_count), f32),
        in_specs=[smem] * 8 + [vmem] * 2,
        out_specs=vmem,
        scratch_shapes=[
            pltpu.VMEM((tile_count, 8, 128), jnp.int32),
            pltpu.VMEM((total, 128, 128), bf16),
            pltpu.VMEM((nblocks, 2 * ch + 16, 128), bf16),
            pltpu.VMEM((edge_blocks + 1, 2 * ch + 16, 128), bf16),
            pltpu.VMEM((total + 1, ch + 8, 128), f32),
            pltpu.VMEM(wide, f32),
            pltpu.VMEM((ROUNDS,) + wide, f32),
            pltpu.VMEM((ROUNDS,) + wide, f32),
            pltpu.VMEM((ROUNDS,) + wide, f32),
            pltpu.VMEM((ROUNDS,) + wide, f32),
            pltpu.VMEM(deg, f32),
            pltpu.VMEM(deg, f32),
            pltpu.VMEM(deg, f32),
            pltpu.VMEM(deg, f32),
            pltpu.VMEM(deg, f32),
            pltpu.VMEM((nblocks, 8, 128), f32),
            pltpu.VMEM(deg, f32),
            dma((2,)),
            dma((OUT_CHUNKS,)),
            dma((OUT_CHUNKS,)),
            dma((ROUNDS, CHUNKS)),
            dma((ROUNDS, CHUNKS)),
            dma((ROUNDS, CHUNKS)),
            dma((ROUNDS, CHUNKS)),
            dma((4,)),
        ],
        compiler_params=pltpu.CompilerParams(
            collective_id=0, has_side_effects=True, vmem_limit_bytes=48 * 1024 * 1024
        ),
    )(order_e, row_e, keep_e, last_e, order_r, edge_r, keep_r, last_r,
      features.reshape(2, ch, row_count), tiles)
    return out.reshape(channels, row_count)


def solution(mesh):
    return jax.shard_map(
        shards,
        mesh=mesh,
        in_specs=(
            P("chan", ("parts", "node")),
            P(("parts", "node", "rep")),
            P(("parts", "node", "rep")),
            P(("parts", "node", "rep"), None),
            P(("parts", "node", "rep"), None, None),
        ),
        out_specs=P("chan", ("parts", "node")),
        check_vma=False,
    )
```

profile of v0, /device:TPU:0, one launch (start us, length us, event | category | flops | bytes accessed | tf_op | source)
XLA Modules:
  0.0 434.8 jit_solution(5500508997579326582)
XLA Ops:
  0.0 0.0 copy-start.3
  0.0 0.7 fusion.8
  0.7 0.0 copy-done.3
  0.7 0.0 copy-start.2
  0.7 0.1 select_reduce_fusion.6
  0.8 0.6 copy-done.2
  1.4 0.5 collective-permute-start
  1.8 0.8 collective-permute-done
  2.6 0.1 convert_reduce_fusion.3
  2.8 0.1 fusion.5
  2.9 0.1 fusion.4
  3.0 0.1 convert_reduce_fusion.2
  3.1 0.2 fusion
  3.3 0.3 convert_reduce_fusion
  3.7 0.3 select_reduce_fusion.1
  3.9 0.1 select_reduce_fusion.keep_r
  4.1 0.1 select_reduce_fusion.3.keep_e
  4.3 0.0 copy-start
  4.3 1.2 copy-done
  5.5 0.0 copy-start.1
  5.5 1.0 copy-done.1
  6.5 427.3 %shard_map.55 = f32[2,32,4096]{2,1,0:T(8,128)S(1)} custom-call(s32[256]{0:T(256)S(1)} %get-tuple-element.7.order_e, s32[256]{0:T(256)S(1)} %get-tuple-element.6.row_e, f32[256]{0:T(256)S(1)} %select_reduce_fusion.3.keep_e, s32[48]{0:T(128)S(1)} %add_select_fusion.1.last_e, s32[256]{0:T(256)S(1)} %get-tuple-element.11.order_r, ...), custom_call_target="tpu_custom_call" | custom-call | tf_op jit(solution)/shard_map/pallas_call | solution.py:302
  433.8 1.0 copy.7
  (7 shorter events, 0.0 us)
Async XLA Ops:
  0.0 0.7 copy-start.3
  0.7 0.7 copy-start.2
  1.4 1.3 collective-permute-start
  4.3 1.2 copy-start
  5.5 1.0 copy-start.1
where the time goes:
time: 435 us
  Pallas kernels  427 us (98%)
    pallas_call x1, Pallas kernels, shards(): pl.pallas_call(functools.partial(kernel, n_node), out_shape=jax.ShapeDtyp...  427 us
  transfers between devices with their start and end apart: 1, of which 1 were waited for; matrix products, arithmetic and copies ran while one was open for 0% of the time, Pallas kernels for 0%

commit v1 on v0

--- a/solution.py
+++ b/solution.py
@@ -10,7 +10,8 @@
 EB_DEV = 12
 CAP = 6
 ROUNDS = 2
-CHUNKS = 8
+CHUNKS = 12
+HOP = 2
 OUT_CHUNKS = 4
 UNROLL = 8
 MESH = pl.DeviceIdType.MESH
@@ -93,20 +94,27 @@
         rows = 2 * ch + (16 if first else 0)
         dims = (((1,), (1 if transposed else 0,)), ((), ()))
 
-        def step(t, running):
-            product = lax.dot_general(
-                source[source_of[t]][:rows], unp[order[t]], dims,
-                preferred_element_type=jnp.float32,
-            )
-            fresh = product[:ch] + product[ch:2 * ch]
-            if first:
-                fresh = jnp.concatenate([fresh, product[2 * ch:2 * ch + 8]], axis=0)
-            running = running * keep[t] + fresh
-            run_sums[t, :ch + (8 if first else 0)] = running
+        def step(g, running):
+            base = g * UNROLL
+            fresh = []
+            for u in range(UNROLL):
+                product = lax.dot_general(
+                    source[source_of[base + u]][:rows], unp[order[base + u]], dims,
+                    preferred_element_type=jnp.float32,
+                )
+                value = product[:ch] + product[ch:2 * ch]
+                if first:
+                    value = jnp.concatenate([value, product[2 * ch:2 * ch + 8]], axis=0)
+                fresh.append(value)
+            for u in range(UNROLL):
+                running = running * keep[base + u] + fresh[u]
+                fresh[u] = running
+            for u in range(UNROLL):
+                run_sums[base + u, :ch + (8 if first else 0)] = fresh[u]
             return running
 
         start = jnp.zeros((ch + (8 if first else 0), 128), jnp.float32)
-        lax.fori_loop(0, total_tiles, step, start, unroll=UNROLL)
+        lax.fori_loop(0, total_tiles // UNROLL, step, start)
 
     def remote(source, target, send, recv, where):
         return pltpu.make_async_remote_copy(
@@ -114,13 +122,18 @@
             device_id={"node": where}, device_id_type=MESH,
         )
 
-    def chunk_copies(turn, k):
+    def copy_right(turn, k):
         part = pl.ds(k * per, per)
-        go_right = remote(to_right.at[turn, part], in_left.at[turn, part],
-                          send_r.at[turn, k], recv_l.at[turn, k], right)
-        go_left = remote(to_left.at[turn, part], in_right.at[turn, part],
-                         send_l.at[turn, k], recv_r.at[turn, k], left)
-        return part, go_right, go_left
+        return remote(to_right.at[turn, part], in_left.at[turn, part],
+                      send_r.at[turn, k], recv_l.at[turn, k], right)
+
+    def copy_left(turn, k):
+        part = pl.ds(k * per, per)
+        return remote(to_left.at[turn, part], in_right.at[turn, part],
+                      send_l.at[turn, k], recv_r.at[turn, k], left)
+
+    deg_right_copy = remote(deg_to_right, deg_left, deg_sem.at[0], deg_sem.at[1], right)
+    deg_left_copy = remote(deg_to_left, deg_right, deg_sem.at[2], deg_sem.at[3], left)
 
     def zero_ends(turn):
         @pl.when(jnp.logical_not(has_left))
@@ -133,53 +146,47 @@
             in_right[turn] = jnp.zeros(in_right.shape[1:], jnp.float32)
             deg_right[...] = jnp.zeros_like(deg_right)
 
-    def forward(turn, k):
-        part, go_right, go_left = chunk_copies(turn, k)
-
-        @pl.when(has_left)
+    def pass_on(turn, k, first, sends, receives, copy_of, to_there, from_there, deg_copy,
+                deg_to_there, deg_from_there):
+        part = pl.ds(k * per, per)
+
+        def degrees_too(act):
+            if first:
+                pl.when(k == 0)(act)
+
+        @pl.when(receives)
         def _():
-            go_right.wait_recv()
-
-        @pl.when(has_right)
+            degrees_too(lambda: deg_copy.wait_recv())
+            copy_of(turn, k).wait_recv()
+
+        @pl.when(sends)
         def _():
-            to_right[turn, part] = own[part] + in_left[turn, part]
-            go_right.start()
-            go_left.wait_recv()
-
-        @pl.when(has_left)
-        def _():
-            to_left[turn, part] = own[part] + in_right[turn, part]
-            go_left.start()
-
-    def forward_degrees():
-        go_right = remote(deg_to_right, deg_left, deg_sem.at[0], deg_sem.at[1], right)
-        go_left = remote(deg_to_left, deg_right, deg_sem.at[2], deg_sem.at[3], left)
-
-        @pl.when(has_left)
-        def _():
-            go_right.wait_recv()
-
-        @pl.when(has_right)
-        def _():
-            deg_to_right[...] = own_deg[...] + deg_left[...]
-            go_right.start()
-            go_left.wait_recv()
-
-        @pl.when(has_left)
-        def _():
-            deg_to_left[...] = own_deg[...] + deg_right[...]
-            go_left.start()
-
-        degree = own_deg[...] + deg_left[...] + deg_right[...]
-        edge_inv[...] = 1.0 / jnp.maximum(degree, 1.0)
-
-        @pl.when(has_right)
-        def _():
-            go_right.wait_send()
-
-        @pl.when(has_left)
-        def _():
-            go_left.wait_send()
+            def send_degrees():
+                deg_to_there[...] = own_deg[...] + deg_from_there[...]
+                deg_copy.start()
+
+            degrees_too(send_degrees)
+            to_there[turn, part] = own[part] + from_there[turn, part]
+            copy_of(turn, k).start()
+
+    def exchange(turn, first):
+        def step(s, _):
+            k_right = s - HOP * pos
+            k_left = s - HOP * (n_node - 1 - pos)
+
+            @pl.when((k_right >= 0) & (k_right < CHUNKS))
+            def _():
+                pass_on(turn, k_right, first, has_right, has_left, copy_right, to_right, in_left,
+                        deg_right_copy, deg_to_right, deg_left)
+
+            @pl.when((k_left >= 0) & (k_left < CHUNKS))
+            def _():
+                pass_on(turn, k_left, first, has_left, has_right, copy_left, to_left, in_right,
+                        deg_left_copy, deg_to_left, deg_right)
+
+            return 0
+
+        lax.fori_loop(0, CHUNKS + HOP * (n_node - 1), step, 0)
 
     for turn in range(ROUNDS):
         first = turn == 0
@@ -190,18 +197,18 @@
             found = run_sums[last_e[b]]
             own[b] = found[:ch]
             if first:
-                own_deg[b] = found[ch:ch + 8]
+                own_deg[pl.ds(b, 1)] = found[ch:ch + 1]
             return 0
 
         lax.fori_loop(0, edge_blocks, take_edges, 0, unroll=4)
+        exchange(turn, first)
         if first:
-            forward_degrees()
-        for k in range(CHUNKS):
-            forward(turn, k)
+            degree = own_deg[...] + deg_left[...] + deg_right[...]
+            edge_inv[...] = 1.0 / jnp.maximum(degree, 1.0)
 
         def means(b, _, turn=turn, first=first):
             edge_sum = own[b] + in_left[turn, b] + in_right[turn, b]
-            ms[b] = split_rows(edge_sum * edge_inv[b, :1], True)
+            ms[b] = split_rows(edge_sum * edge_inv[pl.ds(b, 1)], True)
             return 0
 
         lax.fori_loop(0, edge_blocks, means, 0, unroll=2)
@@ -209,16 +216,26 @@
             [jnp.zeros((2 * ch, 128), jnp.float32), jnp.ones((16, 128), jnp.float32)], axis=0
         ).astype(jnp.bfloat16)
 
-        for k in range(CHUNKS):
-            part, go_right, go_left = chunk_copies(turn, k)
-
+        def sent(k, _, turn=turn):
             @pl.when(has_right)
             def _():
-                go_right.wait_send()
+                copy_right(turn, k).wait_send()
 
             @pl.when(has_left)
             def _():
-                go_left.wait_send()
+                copy_left(turn, k).wait_send()
+
+            return 0
+
+        lax.fori_loop(0, CHUNKS, sent, 0)
+        if first:
+            @pl.when(has_right)
+            def _():
+                deg_right_copy.wait_send()
+
+            @pl.when(has_left)
+            def _():
+                deg_left_copy.wait_send()
 
         sweep(order_r, edge_r, keep_r, ms, True, first)
 
@@ -297,7 +314,7 @@
     vmem = pl.BlockSpec(memory_space=pltpu.VMEM)
     f32, bf16 = jnp.float32, jnp.bfloat16
     wide = (edge_blocks, ch, 128)
-    deg = (edge_blocks, 8, 128)
+    deg = (edge_blocks, 128)
     dma = pltpu.SemaphoreType.DMA
     out = pl.pallas_call(
         functools.partial(kernel, n_node),

time: 435 us -> 111 us (0.26)
  Pallas kernels: 427 us -> 103 us
    pallas_call x1, Pallas kernels: 427 us -> 103 us  [shards(): pl.pallas_call(functools.partial(kernel, n_node), out_shape=jax.ShapeDtyp...]
where the time goes in v1:
time: 111 us
  Pallas kernels  103 us (93%)
  local copies, waits for them, and re-layouts  3.8 us (3%)
  other arithmetic  2.36 us (2%)
    pallas_call x1, Pallas kernels, shards(): pl.pallas_call(functools.partial(kernel, n_node), out_shape=jax.ShapeDtyp...  103 us
    unnamed x9, local copies, waits for them, and re-layouts  3.8 us
  transfers between devices with their start and end apart: 1, of which 1 were waited for; matrix products, arithmetic and copies ran while one was open for 0% of the time, Pallas kernels for 0%

profile of v1, /device:TPU:0, one launch (start us, length us, event | category | flops | bytes accessed | tf_op | source)
XLA Modules:
  0.0 110.7 jit_solution(4985072294612372550)
XLA Ops:
  0.0 0.0 copy-start.3
  0.0 0.7 fusion.8
  0.7 0.0 copy-done.3
  0.7 0.0 copy-start.2
  0.7 0.1 select_reduce_fusion.6
  0.8 0.6 copy-done.2
  1.4 0.5 collective-permute-start
  1.8 0.8 collective-permute-done
  2.6 0.1 convert_reduce_fusion.3
  2.8 0.1 fusion.5
  2.9 0.1 fusion.4
  3.0 0.1 convert_reduce_fusion.2
  3.1 0.2 fusion
  3.3 0.3 convert_reduce_fusion
  3.7 0.3 select_reduce_fusion.1
  3.9 0.1 select_reduce_fusion.keep_r
  4.1 0.1 select_reduce_fusion.3.keep_e
  4.3 0.0 copy-start
  4.3 1.2 %copy-done = f32[64,4096]{1,0:T(8,128)S(1)} copy-done((f32[64,4096]{1,0:T(8,128)S(1)}, f32[64,4096]{1,0:T(8,128)}, u32[]{:S(2)}) %copy-start) | copy-done | bytes 1048600
  5.5 0.0 copy-start.1
  5.5 1.0 copy-done.1
  6.5 103.2 %shard_map.55 = f32[2,32,4096]{2,1,0:T(8,128)S(1)} custom-call(s32[256]{0:T(256)S(1)} %get-tuple-element.7.order_e, s32[256]{0:T(256)S(1)} %get-tuple-element.6.row_e, f32[256]{0:T(256)S(1)} %select_reduce_fusion.3.keep_e, s32[48]{0:T(128)S(1)} %add_select_fusion.1.last_e, s32[256]{0:T(256)S(1)} %get-tuple-element.11.order_r, ...), custom_call_target="tpu_custom_call" | custom-call | tf_op jit(solution)/shard_map/pallas_call | solution.py:319
  109.7 1.0 copy.7
  (7 shorter events, 0.0 us)
Async XLA Ops:
  0.0 0.7 copy-start.3
  0.7 0.7 copy-start.2
  1.4 1.3 %collective-permute-start = (s32[256]{0:T(256)S(1)}, s32[256]{0:T(256)S(1)}, u32[]{:S(2)}, u32[]{:S(2)}) collective-permute-start(s32[256]{0:T(256)S(1)} %pad_add_fusion.1), channel_id=1, source_target_pairs={{0,1},{1,0},{2,3},{3,2},{4,5},{5,4},{6,7},{7,6},{8,9},{9,8},{10,11... | collective-permute-start | bytes 3080 | tf_op jit(solution)/shard_map/ppermute | solution.py:292
  4.3 1.2 %copy-start = (f32[64,4096]{1,0:T(8,128)S(1)}, f32[64,4096]{1,0:T(8,128)}, u32[]{:S(2)}) copy-start(f32[64,4096]{1,0:T(8,128)} %param.5) | copy-start | bytes 3145732
  5.5 1.0 copy-start.1

commit v2 on v1

--- a/solution.py
+++ b/solution.py
@@ -10,10 +10,10 @@
 EB_DEV = 12
 CAP = 6
 ROUNDS = 2
-CHUNKS = 12
-HOP = 2
-OUT_CHUNKS = 4
-UNROLL = 8
+CHUNKS = 16
+HOP = 8
+OUT_CHUNKS = 2
+UNROLL = 32
 MESH = pl.DeviceIdType.MESH
 teleport = 0.1
 
@@ -35,11 +35,11 @@
     own_deg, deg_left, deg_right, deg_to_left, deg_to_right, node_floor, edge_inv,
     tile_sem, out_send, out_recv, send_l, send_r, recv_l, recv_r, deg_sem,
 ):
-    ch = feat_ref.shape[1]
+    halves, ch = feat_ref.shape[1:3]
     tile_count = tiles_ref.shape[0]
     total_tiles = 2 * tile_count
-    nblocks = feat_ref.shape[2] // 128
-    edge_blocks = own.shape[0]
+    nblocks = feat_ref.shape[3] // 128
+    edge_blocks = own.shape[1]
     per = edge_blocks // CHUNKS
     pos = lax.axis_index("node")
     rep = lax.axis_index("rep")
@@ -81,8 +81,9 @@
         lax.fori_loop(0, tile_count, body, 0, unroll=4)
 
     def load_features(r, _):
-        block = feat_ref[rep, :, pl.ds(pl.multiple_of(r * 128, 128), 128)]
-        xs[r] = split_rows(block, True)
+        for h in range(halves):
+            block = feat_ref[rep, h, :, pl.ds(pl.multiple_of(r * 128, 128), 128)]
+            xs[h, r] = split_rows(block, True)
         return 0
 
     lax.fori_loop(0, nblocks, load_features, 0, unroll=2)
@@ -90,7 +91,7 @@
     tile_copy.wait()
     unpack_from(tiles_in, tile_count)
 
-    def sweep(order, source_of, keep, source, transposed, first):
+    def sweep(order, source_of, keep, source, h, transposed, first, span=None):
         rows = 2 * ch + (16 if first else 0)
         dims = (((1,), (1 if transposed else 0,)), ((), ()))
 
@@ -99,7 +100,7 @@
             fresh = []
             for u in range(UNROLL):
                 product = lax.dot_general(
-                    source[source_of[base + u]][:rows], unp[order[base + u]], dims,
+                    source[h, source_of[base + u]][:rows], unp[order[base + u]], dims,
                     preferred_element_type=jnp.float32,
                 )
                 value = product[:ch] + product[ch:2 * ch]
@@ -114,7 +115,18 @@
             return running
 
         start = jnp.zeros((ch + (8 if first else 0), 128), jnp.float32)
-        lax.fori_loop(0, total_tiles // UNROLL, step, start)
+        groups = total_tiles // UNROLL
+        if span is None:
+            lax.fori_loop(0, groups, step, start)
+            return
+        phase, low, high = span
+        count = high - low
+
+        def outer(s, running):
+            exchange_step(phase, low + s)
+            return lax.fori_loop(s * groups // count, (s + 1) * groups // count, step, running)
+
+        lax.fori_loop(0, count, outer, start)
 
     def remote(source, target, send, recv, where):
         return pltpu.make_async_remote_copy(
@@ -135,18 +147,7 @@
     deg_right_copy = remote(deg_to_right, deg_left, deg_sem.at[0], deg_sem.at[1], right)
     deg_left_copy = remote(deg_to_left, deg_right, deg_sem.at[2], deg_sem.at[3], left)
 
-    def zero_ends(turn):
-        @pl.when(jnp.logical_not(has_left))
-        def _():
-            in_left[turn] = jnp.zeros(in_left.shape[1:], jnp.float32)
-            deg_left[...] = jnp.zeros_like(deg_left)
-
-        @pl.when(jnp.logical_not(has_right))
-        def _():
-            in_right[turn] = jnp.zeros(in_right.shape[1:], jnp.float32)
-            deg_right[...] = jnp.zeros_like(deg_right)
-
-    def pass_on(turn, k, first, sends, receives, copy_of, to_there, from_there, deg_copy,
+    def pass_on(turn, h, k, first, sends, receives, copy_of, to_there, from_there, deg_copy,
                 deg_to_there, deg_from_there):
         part = pl.ds(k * per, per)
 
@@ -166,113 +167,174 @@
                 deg_copy.start()
 
             degrees_too(send_degrees)
-            to_there[turn, part] = own[part] + from_there[turn, part]
+            to_there[turn, part] = own[h, part] + from_there[turn, part]
             copy_of(turn, k).start()
 
-    def exchange(turn, first):
-        def step(s, _):
-            k_right = s - HOP * pos
-            k_left = s - HOP * (n_node - 1 - pos)
-
-            @pl.when((k_right >= 0) & (k_right < CHUNKS))
-            def _():
-                pass_on(turn, k_right, first, has_right, has_left, copy_right, to_right, in_left,
-                        deg_right_copy, deg_to_right, deg_left)
-
-            @pl.when((k_left >= 0) & (k_left < CHUNKS))
-            def _():
-                pass_on(turn, k_left, first, has_left, has_right, copy_left, to_left, in_right,
-                        deg_left_copy, deg_to_left, deg_right)
-
+    def go_right(phase, k):
+        pass_on(phase, phase % halves, k, phase == 0, has_right, has_left, copy_right, to_right,
+                in_left, deg_right_copy, deg_to_right, deg_left)
+
+    def go_left(phase, k):
+        pass_on(phase, phase % halves, k, phase == 0, has_left, has_right, copy_left, to_left,
+                in_right, deg_left_copy, deg_to_left, deg_right)
+
+    def every_chunk(move, phase):
+        def one(k, _):
+            move(phase, k)
             return 0
 
-        lax.fori_loop(0, CHUNKS + HOP * (n_node - 1), step, 0)
-
-    for turn in range(ROUNDS):
-        first = turn == 0
-        zero_ends(turn)
-        sweep(order_e, row_e, keep_e, xs, False, first)
-
-        def take_edges(b, _, first=first):
+        lax.fori_loop(0, CHUNKS, one, 0)
+
+    def exchange_start(phase):
+        pl.when(jnp.logical_not(has_left))(lambda: every_chunk(go_right, phase))
+        pl.when(jnp.logical_not(has_right))(lambda: every_chunk(go_left, phase))
+
+    def exchange_step(phase, s):
+        k_right = s - HOP * (pos - 1)
+        k_left = s - HOP * (n_node - 2 - pos)
+        inner = has_left & has_right
+
+        @pl.when(inner & (k_right >= 0) & (k_right < CHUNKS))
+        def _():
+            go_right(phase, k_right)
+
+        @pl.when(inner & (k_left >= 0) & (k_left < CHUNKS))
+        def _():
+            go_left(phase, k_left)
+
+    def exchange_end(phase):
+        pl.when(jnp.logical_not(has_right))(lambda: every_chunk(go_right, phase))
+        pl.when(jnp.logical_not(has_left))(lambda: every_chunk(go_left, phase))
+
+    steps = CHUNKS + HOP * max(n_node - 2, 0)
+
+    def push(turn, h, span=None):
+        first = turn == 0 and h == 0
+        sweep(order_e, row_e, keep_e, xs, h, False, first, span)
+
+        def take_edges(b, _):
             found = run_sums[last_e[b]]
-            own[b] = found[:ch]
+            own[h, b] = found[:ch]
             if first:
                 own_deg[pl.ds(b, 1)] = found[ch:ch + 1]
             return 0
 
         lax.fori_loop(0, edge_blocks, take_edges, 0, unroll=4)
-        exchange(turn, first)
+        exchange_start(turn * halves + h)
+
+    def pull(turn, h, span=None):
+        first = turn == 0 and h == 0
+        phase = turn * halves + h
+        exchange_end(phase)
         if first:
             degree = own_deg[...] + deg_left[...] + deg_right[...]
             edge_inv[...] = 1.0 / jnp.maximum(degree, 1.0)
 
-        def means(b, _, turn=turn, first=first):
-            edge_sum = own[b] + in_left[turn, b] + in_right[turn, b]
-            ms[b] = split_rows(edge_sum * edge_inv[pl.ds(b, 1)], True)
+        def means(b, _):
+            edge_sum = own[h, b] + in_left[phase, b] + in_right[phase, b]
+            ms[h, b] = split_rows(edge_sum * edge_inv[pl.ds(b, 1)], True)
             return 0
 
-        lax.fori_loop(0, edge_blocks, means, 0, unroll=2)
-        ms[edge_blocks] = jnp.concatenate(
-            [jnp.zeros((2 * ch, 128), jnp.float32), jnp.ones((16, 128), jnp.float32)], axis=0
-        ).astype(jnp.bfloat16)
-
-        def sent(k, _, turn=turn):
-            @pl.when(has_right)
-            def _():
-                copy_right(turn, k).wait_send()
-
-            @pl.when(has_left)
-            def _():
-                copy_left(turn, k).wait_send()
-
-            return 0
-
-        lax.fori_loop(0, CHUNKS, sent, 0)
-        if first:
-            @pl.when(has_right)
-            def _():
-                deg_right_copy.wait_send()
-
-            @pl.when(has_left)
-            def _():
-                deg_left_copy.wait_send()
-
-        sweep(order_r, edge_r, keep_r, ms, True, first)
-
-        def new_block(r, first=first):
+        lax.fori_loop(0, edge_blocks, means, 0, unroll=4)
+        sweep(order_r, edge_r, keep_r, ms, h, True, first, span)
+
+        def new_block(r):
             found = run_sums[last_r[r]]
             if first:
                 node_floor[r] = jnp.maximum(found[ch:ch + 8], 1.0)
             lanes = pl.ds(pl.multiple_of(r * 128, 128), 128)
-            block = feat_ref[rep, :, lanes]
+            block = feat_ref[rep, h, :, lanes]
             return lanes, (1.0 - teleport) * (found[:ch] / node_floor[r][:1]) + teleport * block
 
         if turn < ROUNDS - 1:
             def next_x(r, _):
-                xs[r] = split_rows(new_block(r)[1], True)
+                xs[h, r] = split_rows(new_block(r)[1], True)
                 return 0
 
-            lax.fori_loop(0, nblocks, next_x, 0, unroll=2)
-        else:
-            group = nblocks // OUT_CHUNKS
-            copies = []
-            for k in range(OUT_CHUNKS):
-                def last_x(r, _):
-                    lanes, value = new_block(r)
-                    out_ref[rep, :, lanes] = value
-                    return 0
-
-                lax.fori_loop(k * group, (k + 1) * group, last_x, 0, unroll=2)
-                span = pl.ds(k * group * 128, group * 128)
-                copy = pltpu.make_async_remote_copy(
-                    src_ref=out_ref.at[rep, :, span], dst_ref=out_ref.at[rep, :, span],
-                    send_sem=out_send.at[k], recv_sem=out_recv.at[k],
-                    device_id={"rep": 1 - rep}, device_id_type=MESH,
-                )
-                copy.start()
-                copies.append(copy)
-            for copy in copies:
-                copy.wait()
+            lax.fori_loop(0, nblocks, next_x, 0, unroll=4)
+            return []
+        group = nblocks // OUT_CHUNKS
+        copies = []
+        for k in range(OUT_CHUNKS):
+            def last_x(r, _):
+                lanes, value = new_block(r)
+                out_ref[rep, h, :, lanes] = value
+                return 0
+
+            lax.fori_loop(k * group, (k + 1) * group, last_x, 0, unroll=4)
+            lanes = pl.ds(k * group * 128, group * 128)
+            copy = pltpu.make_async_remote_copy(
+                src_ref=out_ref.at[rep, h, :, lanes], dst_ref=out_ref.at[rep, h, :, lanes],
+                send_sem=out_send.at[h, k], recv_sem=out_recv.at[h, k],
+                device_id={"rep": 1 - rep}, device_id_type=MESH,
+            )
+            copy.start()
+            copies.append(copy)
+        return copies
+
+    @pl.when(jnp.logical_not(has_left))
+    def _():
+        in_left[...] = jnp.zeros_like(in_left)
+        deg_left[...] = jnp.zeros_like(deg_left)
+
+    @pl.when(jnp.logical_not(has_right))
+    def _():
+        in_right[...] = jnp.zeros_like(in_right)
+        deg_right[...] = jnp.zeros_like(deg_right)
+
+    for h in range(halves):
+        ms[h, edge_blocks] = jnp.concatenate(
+            [jnp.zeros((2 * ch, 128), jnp.float32), jnp.ones((16, 128), jnp.float32)], axis=0
+        ).astype(jnp.bfloat16)
+
+    copies = []
+    if halves == 1:
+        for turn in range(ROUNDS):
+            push(turn, 0)
+
+            def alone(s, _, turn=turn):
+                exchange_step(turn, s)
+                return 0
+
+            lax.fori_loop(0, steps, alone, 0)
+            copies += pull(turn, 0)
+    else:
+        cut = steps // 2
+        push(0, 0)
+        push(0, 1, (0, 0, steps))
+        for turn in range(ROUNDS):
+            for h in range(2):
+                phase = 2 * turn + h + 1
+                if turn < ROUNDS - 1:
+                    copies += pull(turn, h, (phase, 0, cut))
+                    push(turn + 1, h, (phase, cut, steps))
+                else:
+                    copies += pull(turn, h, (phase, 0, steps) if h == 0 else None)
+
+    for phase in range(ROUNDS * halves):
+        def sent(k, _, phase=phase):
+            @pl.when(has_right)
+            def _():
+                copy_right(phase, k).wait_send()
+
+            @pl.when(has_left)
+            def _():
+                copy_left(phase, k).wait_send()
+
+            return 0
+
+        lax.fori_loop(0, CHUNKS, sent, 0)
+
+    @pl.when(has_right)
+    def _():
+        deg_right_copy.wait_send()
+
+    @pl.when(has_left)
+    def _():
+        deg_left_copy.wait_send()
+
+    for copy in copies:
+        copy.wait()
 
 
 def shards(features, tile_rows, tile_slot, slot_block, tiles):
@@ -281,7 +343,9 @@
     nblocks = row_count // 128
     tile_count = tile_rows.shape[0]
     total = 2 * tile_count
-    ch = channels // 2
+    halves = 2 if channels % 32 == 0 else 1
+    ch = channels // 2 // halves
+    phases = ROUNDS * halves
     edge_blocks = n_node * EB_DEV
 
     slots = slot_block.reshape(-1)
@@ -318,20 +382,20 @@
     dma = pltpu.SemaphoreType.DMA
     out = pl.pallas_call(
         functools.partial(kernel, n_node),
-        out_shape=jax.ShapeDtypeStruct((2, ch, row_count), f32),
+        out_shape=jax.ShapeDtypeStruct((2, halves, ch, row_count), f32),
         in_specs=[smem] * 8 + [vmem] * 2,
         out_specs=vmem,
         scratch_shapes=[
             pltpu.VMEM((tile_count, 8, 128), jnp.int32),
             pltpu.VMEM((total, 128, 128), bf16),
-            pltpu.VMEM((nblocks, 2 * ch + 16, 128), bf16),
-            pltpu.VMEM((edge_blocks + 1, 2 * ch + 16, 128), bf16),
+            pltpu.VMEM((halves, nblocks, 2 * ch + 16, 128), bf16),
+            pltpu.VMEM((halves, edge_blocks + 1, 2 * ch + 16, 128), bf16),
             pltpu.VMEM((total + 1, ch + 8, 128), f32),
-            pltpu.VMEM(wide, f32),
-            pltpu.VMEM((ROUNDS,) + wide, f32),
-            pltpu.VMEM((ROUNDS,) + wide, f32),
-            pltpu.VMEM((ROUNDS,) + wide, f32),
-            pltpu.VMEM((ROUNDS,) + wide, f32),
+            pltpu.VMEM((halves,) + wide, f32),
+            pltpu.VMEM((phases,) + wide, f32),
+            pltpu.VMEM((phases,) + wide, f32),
+            pltpu.VMEM((phases,) + wide, f32),
+            pltpu.VMEM((phases,) + wide, f32),
             pltpu.VMEM(deg, f32),
             pltpu.VMEM(deg, f32),
             pltpu.VMEM(deg, f32),
@@ -340,19 +404,19 @@
             pltpu.VMEM((nblocks, 8, 128), f32),
             pltpu.VMEM(deg, f32),
             dma((2,)),
-            dma((OUT_CHUNKS,)),
-            dma((OUT_CHUNKS,)),
-            dma((ROUNDS, CHUNKS)),
-            dma((ROUNDS, CHUNKS)),
-            dma((ROUNDS, CHUNKS)),
-            dma((ROUNDS, CHUNKS)),
+            dma((halves, OUT_CHUNKS)),
+            dma((halves, OUT_CHUNKS)),
+            dma((phases, CHUNKS)),
+            dma((phases, CHUNKS)),
+            dma((phases, CHUNKS)),
+            dma((phases, CHUNKS)),
             dma((4,)),
         ],
         compiler_params=pltpu.CompilerParams(
             collective_id=0, has_side_effects=True, vmem_limit_bytes=48 * 1024 * 1024
         ),
     )(order_e, row_e, keep_e, last_e, order_r, edge_r, keep_r, last_r,
-      features.reshape(2, ch, row_count), tiles)
+      features.reshape(2, halves, ch, row_count), tiles)
     return out.reshape(channels, row_count)
 
 

time: 111 us -> 84.4 us (0.76)
  Pallas kernels: 103 us -> 76.8 us
    pallas_call x1, Pallas kernels: 103 us -> 76.8 us  [shards(): pl.pallas_call(functools.partial(kernel, n_node), out_shape=jax.ShapeDtyp...]
where the time goes in v2:
time: 84.4 us; the launch traced here: 84.3 us
  Pallas kernels  76.8 us (91%)
  local copies, waits for them, and re-layouts  3.8 us (5%)
  other arithmetic  2.36 us (3%)
    pallas_call x1, Pallas kernels, shards(): pl.pallas_call(functools.partial(kernel, n_node), out_shape=jax.ShapeDtyp...  76.8 us
    unnamed x9, local copies, waits for them, and re-layouts  3.8 us
  transfers between devices with their start and end apart: 1, of which 1 were waited for; matrix products, arithmetic and copies ran while one was open for 0% of the time, Pallas kernels for 0%

profile of v2, /device:TPU:0, one launch (start us, length us, event | category | flops | bytes accessed | tf_op | source)
XLA Modules:
  0.0 84.3 jit_solution(6094048050502986394)
XLA Ops:
  0.0 0.0 copy-start.3
  0.0 0.7 fusion.8
  0.7 0.0 copy-done.3
  0.7 0.0 copy-start.2
  0.7 0.1 select_reduce_fusion.6
  0.8 0.6 copy-done.2
  1.4 0.5 collective-permute-start
  1.8 0.8 collective-permute-done
  2.6 0.1 convert_reduce_fusion.3
  2.8 0.1 fusion.5
  2.9 0.1 fusion.4
  3.0 0.1 convert_reduce_fusion.2
  3.1 0.2 fusion
  3.3 0.3 convert_reduce_fusion
  3.7 0.3 select_reduce_fusion.1
  3.9 0.1 select_reduce_fusion.keep_r
  4.1 0.1 select_reduce_fusion.3.keep_e
  4.3 0.0 copy-start
  4.3 1.2 %copy-done = f32[64,4096]{1,0:T(8,128)S(1)} copy-done((f32[64,4096]{1,0:T(8,128)S(1)}, f32[64,4096]{1,0:T(8,128)}, u32[]{:S(2)}) %copy-start) | copy-done | bytes 1048600
  5.5 0.0 copy-start.1
  5.5 1.0 %copy-done.1 = s32[128,8,128]{2,1,0:T(8,128)S(1)} copy-done((s32[128,8,128]{2,1,0:T(8,128)S(1)}, s32[128,8,128]{2,1,0:T(8,128)}, u32[]{:S(2)}) %copy-start.1) | copy-done | bytes 524312
  6.5 76.8 %shard_map.55 = f32[2,2,16,4096]{3,2,1,0:T(8,128)S(1)} custom-call(s32[256]{0:T(256)S(1)} %get-tuple-element.7.order_e, s32[256]{0:T(256)S(1)} %get-tuple-element.6.row_e, f32[256]{0:T(256)S(1)} %select_reduce_fusion.3.keep_e, s32[48]{0:T(128)S(1)} %add_select_fusion.1.last_e, s32[256]{0:T(256)S(1)} %get-tuple-element.11.order_r, ...), custom_call_target="tpu_custom_call" | custom-call | tf_op jit(solution)/shard_map/pallas_call | solution.py:383
  83.3 1.0 %copy.7 = f32[64,4096]{1,0:T(8,128)} copy(f32[64,4096]{1,0:T(8,128)S(1)} %bitcast.4) | data formatting | bytes 2097152
  (7 shorter events, 0.0 us)
Async XLA Ops:
  0.0 0.7 copy-start.3
  0.7 0.7 copy-start.2
  1.4 1.3 %collective-permute-start = (s32[256]{0:T(256)S(1)}, s32[256]{0:T(256)S(1)}, u32[]{:S(2)}, u32[]{:S(2)}) collective-permute-start(s32[256]{0:T(256)S(1)} %pad_add_fusion.1), channel_id=1, source_target_pairs={{0,1},{1,0},{2,3},{3,2},{4,5},{5,4},{6,7},{7,6},{8,9},{9,8},{10,11... | collective-permute-start | bytes 3080 | tf_op jit(solution)/shard_map/ppermute | solution.py:356
  4.3 1.2 %copy-start = (f32[64,4096]{1,0:T(8,128)S(1)}, f32[64,4096]{1,0:T(8,128)}, u32[]{:S(2)}) copy-start(f32[64,4096]{1,0:T(8,128)} %param.5) | copy-start | bytes 3145732
  5.5 1.0 %copy-start.1 = (s32[128,8,128]{2,1,0:T(8,128)S(1)}, s32[128,8,128]{2,1,0:T(8,128)}, u32[]{:S(2)}) copy-start(s32[128,8,128]{2,1,0:T(8,128)} %tiles_ref.1) | copy-start | bytes 1572868

commit v3 on v2

--- a/solution.py
+++ b/solution.py
@@ -10,8 +10,8 @@
 EB_DEV = 12
 CAP = 6
 ROUNDS = 2
-CHUNKS = 16
-HOP = 8
+CHUNKS = 8
+HOP = 6
 OUT_CHUNKS = 2
 UNROLL = 32
 MESH = pl.DeviceIdType.MESH

time: 84.4 us -> 85.2 us (level)
  no operation moved by 1% of the time
where the time goes in v3:
time: 85.2 us; the launch traced here: 85 us
  Pallas kernels  77.5 us (91%)
  local copies, waits for them, and re-layouts  3.8 us (4%)
  other arithmetic  2.36 us (3%)
    pallas_call x1, Pallas kernels, shards(): pl.pallas_call(functools.partial(kernel, n_node), out_shape=jax.ShapeDtyp...  77.5 us
    unnamed x9, local copies, waits for them, and re-layouts  3.8 us
  transfers between devices with their start and end apart: 1, of which 1 were waited for; matrix products, arithmetic and copies ran while one was open for 0% of the time, Pallas kernels for 0%

profile of v3, /device:TPU:0, one launch (start us, length us, event | category | flops | bytes accessed | tf_op | source)
XLA Modules:
  0.0 85.0 jit_solution(11488061409303743121)
XLA Ops:
  0.0 0.0 copy-start.3
  0.0 0.7 fusion.8
  0.7 0.0 copy-done.3
  0.7 0.0 copy-start.2
  0.7 0.1 select_reduce_fusion.6
  0.8 0.6 copy-done.2
  1.4 0.5 collective-permute-start
  1.8 0.8 collective-permute-done
  2.6 0.1 convert_reduce_fusion.3
  2.8 0.1 fusion.5
  2.9 0.1 fusion.4
  3.0 0.1 convert_reduce_fusion.2
  3.1 0.2 fusion
  3.3 0.3 convert_reduce_fusion
  3.7 0.3 select_reduce_fusion.1
  3.9 0.1 select_reduce_fusion.keep_r
  4.1 0.1 select_reduce_fusion.3.keep_e
  4.3 0.0 copy-start
  4.3 1.2 %copy-done = f32[64,4096]{1,0:T(8,128)S(1)} copy-done((f32[64,4096]{1,0:T(8,128)S(1)}, f32[64,4096]{1,0:T(8,128)}, u32[]{:S(2)}) %copy-start) | copy-done | bytes 1048600
  5.5 0.0 copy-start.1
  5.5 1.0 %copy-done.1 = s32[128,8,128]{2,1,0:T(8,128)S(1)} copy-done((s32[128,8,128]{2,1,0:T(8,128)S(1)}, s32[128,8,128]{2,1,0:T(8,128)}, u32[]{:S(2)}) %copy-start.1) | copy-done | bytes 524312
  6.5 77.5 %shard_map.55 = f32[2,2,16,4096]{3,2,1,0:T(8,128)S(1)} custom-call(s32[256]{0:T(256)S(1)} %get-tuple-element.7.order_e, s32[256]{0:T(256)S(1)} %get-tuple-element.6.row_e, f32[256]{0:T(256)S(1)} %select_reduce_fusion.3.keep_e, s32[48]{0:T(128)S(1)} %add_select_fusion.1.last_e, s32[256]{0:T(256)S(1)} %get-tuple-element.11.order_r, ...), custom_call_target="tpu_custom_call" | custom-call | tf_op jit(solution)/shard_map/pallas_call | solution.py:383
  84.0 1.0 %copy.7 = f32[64,4096]{1,0:T(8,128)} copy(f32[64,4096]{1,0:T(8,128)S(1)} %bitcast.4) | data formatting | bytes 2097152
  (7 shorter events, 0.0 us)
Async XLA Ops:
  0.0 0.7 copy-start.3
  0.7 0.7 copy-start.2
  1.4 1.3 %collective-permute-start = (s32[256]{0:T(256)S(1)}, s32[256]{0:T(256)S(1)}, u32[]{:S(2)}, u32[]{:S(2)}) collective-permute-start(s32[256]{0:T(256)S(1)} %pad_add_fusion.1), channel_id=1, source_target_pairs={{0,1},{1,0},{2,3},{3,2},{4,5},{5,4},{6,7},{7,6},{8,9},{9,8},{10,11... | collective-permute-start | bytes 3080 | tf_op jit(solution)/shard_map/ppermute | solution.py:356
  4.3 1.2 %copy-start = (f32[64,4096]{1,0:T(8,128)S(1)}, f32[64,4096]{1,0:T(8,128)}, u32[]{:S(2)}) copy-start(f32[64,4096]{1,0:T(8,128)} %param.5) | copy-start | bytes 3145732
  5.5 1.0 %copy-start.1 = (s32[128,8,128]{2,1,0:T(8,128)S(1)}, s32[128,8,128]{2,1,0:T(8,128)}, u32[]{:S(2)}) copy-start(s32[128,8,128]{2,1,0:T(8,128)} %tiles_ref.1) | copy-start | bytes 1572868
